TPU v7x, 256 devices: a whole 4x4x8 slice. The times are simulated.
256 devices in a mesh: outer: 16 (over z_lo, y, core), inner: 16 (over z_hi, x).
Axes of the slice: x: 4, y: 4, z: 8 (z_hi: 4, z_lo: 2; z = z_hi * 2 + z_lo), core: 2. Of those that a mesh axis runs over, the one named last changes fastest.
Arguments:
- queries: bfloat16 [65536, 4096], P(('outer', 'inner')), may hold values from -300 to 300
- key_codes: bfloat16 [65536, 1024], P(('outer', 'inner')), may hold values from -6 to 6
- value_code_rows: bfloat16 [65536, 1024], P(('outer', 'inner')), may hold values from -6 to 6
- key_span_scales: float32 [512, 8], P(('outer', 'inner')), may hold values from 0.5 to 2
- value_span_scales: float32 [512, 8], P(('outer', 'inner')), may hold values from 0.5 to 2
- formats: int32 [2, 8], replicated, may hold values from 0 to 1
- span_order: int32 [512], replicated, may hold values from 0 to 511, each once
Outputs:
- attended: bfloat16 [65536, 4096], P(('outer', 'inner'))
Inputs may be any that keep to these rules, and one draw needn't show every extreme that they name: `span_order`: each span number appears once.
All inputs are finite; a program needn't handle non-finite values.
Results may differ from a plain program's by a relative error of at most 0.035.
Values may be sent and summed in bfloat16 or wider, within the bound.
A program may use at most 64 MiB of HBM per device.

v0:
```python
import math

import jax
import jax.numpy as jnp
from jax import lax
from jax.sharding import PartitionSpec as P

QUERY_HEADS = 32
KEY_HEADS = 8
HEAD_SIZE = 128
GROUP_QUERIES = 4


def from_behind(array, axis, by):
    count = lax.axis_size(axis)
    return lax.ppermute(array, axis, [(i, (i + by) % count) for i in range(count)])


def for_sending(array):
    return jax.tree.map(lambda a: a.astype(jnp.bfloat16) if a.dtype == jnp.float32 else a, array)


def dequantize(code_matrix, scales, units):
    block_rows = code_matrix.shape[0]
    reshaped_rows = code_matrix.reshape(2, block_rows // 2, KEY_HEADS, HEAD_SIZE).astype(
        jnp.float32
    )
    reshaped_rows = reshaped_rows * scales[:, None, :, None] * units[None, None, :, None]
    return reshaped_rows.astype(jnp.bfloat16).reshape(block_rows, KEY_HEADS, HEAD_SIZE)


def block_positions(span_order, block, block_rows):
    half = block_rows // 2
    slots = lax.dynamic_slice(span_order, (block * 2,), (2,))
    offsets = jnp.arange(half, dtype=jnp.int32)
    return (slots[:, None] * half + offsets[None, :]).reshape(block_rows)


def shards(
    queries, key_codes, value_code_rows, key_span_scales, value_span_scales, formats, span_order
):
    block_rows = queries.shape[0]
    n_outer = lax.axis_size("outer")
    n_inner = lax.axis_size("inner")
    outer_idx = lax.axis_index("outer")
    inner_idx = lax.axis_index("inner")
    units = jnp.where(formats == 0, 1.0, 0.25).astype(jnp.float32)
    own = (key_codes, value_code_rows, key_span_scales, value_span_scales)
    blocks = [own]
    current = own
    for step in range(2):
        current = (
            from_behind(current[0], "inner", 1),
            from_behind(current[1], "inner", 1),
            from_behind(current[2].astype(jnp.bfloat16), "inner", 1).astype(jnp.float32),
            from_behind(current[3].astype(jnp.bfloat16), "inner", 1).astype(jnp.float32),
        )
        blocks.append(current)
    stacked = tuple((jnp.stack([entry[member] for entry in blocks]) for member in range(4)))
    moved = jax.tree.map(
        lambda part, own: part.astype(own.dtype),
        from_behind(for_sending(stacked), "outer", 1),
        stacked,
    )
    blocks = blocks + [tuple((moved[member][which] for member in range(4))) for which in range(3)]
    offsets = [(0, 0), (0, 1), (0, 2), (1, 0), (1, 1), (1, 2)]
    key_rows, value_rows, key_pos = ([], [], [])
    for entry, shift_pair in zip(blocks, offsets):
        source = (outer_idx - shift_pair[0]) % n_outer * n_inner + (
            inner_idx - shift_pair[1]
        ) % n_inner
        key_rows.append(dequantize(entry[0], entry[2], units[0]))
        value_rows.append(dequantize(entry[1], entry[3], units[1]))
        key_pos.append(block_positions(span_order, source, block_rows))
    keys = jnp.concatenate(key_rows, 0).transpose(1, 0, 2)
    values = jnp.concatenate(value_rows, 0).transpose(1, 0, 2)
    kpos = jnp.concatenate(key_pos, 0)
    qpos = block_positions(span_order, outer_idx * n_inner + inner_idx, block_rows)
    allowed = (kpos[None, :] <= qpos[:, None])[None]
    factor = 1.0 / math.sqrt(HEAD_SIZE)
    grouped_queries = queries.reshape(block_rows, KEY_HEADS, GROUP_QUERIES, HEAD_SIZE).transpose(
        1, 0, 2, 3
    )

    def one_head(operands):
        query_head, khead, vhead = operands
        score = (
            jnp.einsum("tgd,cd->gtc", query_head, khead, preferred_element_type=jnp.float32)
            * factor
        )
        masked = jnp.where(allowed, score, -jnp.inf)
        peak = jnp.max(masked, axis=-1, keepdims=True)
        expo = jnp.where(allowed, jnp.exp(masked - peak), 0.0)
        total = jnp.sum(expo, axis=-1)
        weights = expo.astype(jnp.bfloat16)
        summed = jnp.einsum("gtc,cd->tgd", weights, vhead, preferred_element_type=jnp.float32)
        return (summed / total.transpose(1, 0)[..., None]).astype(jnp.bfloat16)

    result = lax.map(one_head, (grouped_queries, keys, values))
    return result.transpose(1, 0, 2, 3).reshape(block_rows, QUERY_HEADS * HEAD_SIZE)


def solution(mesh):
    placed = (
        P(("outer", "inner"), None),
        P(("outer", "inner"), None),
        P(("outer", "inner"), None),
        P(("outer", "inner"), None),
        P(("outer", "inner"), None),
        P(),
        P(),
    )
    return jax.shard_map(
        shards, mesh=mesh, in_specs=placed, out_specs=P(("outer", "inner"), None), check_vma=False
    )
```

profile of v0, /device:TPU:102, one launch (start us, length us, event | category | flops | bytes accessed | tf_op | source)
XLA Modules:
  0.0 235.0 jit_solution(14918114242822897640)
XLA Ops:
  0.0 1.2 copy.23
  1.2 3.6 %collective-permute-start.6 = (bf16[256,1024]{0,1:T(8,128)(2,1)S(1)}, bf16[256,1024]{0,1:T(8,128)(2,1)S(1)}, u32[]{:S(2)}, u32[]{:S(2)}) collective-permute-start(bf16[256,1024]{0,1:T(8,128)(2,1)S(1)} %copy.23), channel_id=1, source_target_pairs={{0,1},{1,2},{2,3},{3,4},{4,5},{5,6},{6,7},{7,8},{8,9},{9,10},{10,1... | collective-permute-start | bytes 1572872 | tf_op jit(solution)/shard_map/ppermute | solution.py:16
  4.8 0.7 convert_element_type.193
  5.5 1.5 collective-permute-start.7
  7.0 1.5 collective-permute-start
  8.5 0.7 convert_element_type.171
  9.2 1.2 collective-permute-start.1
  10.4 0.7 broadcast_bitcast_fusion.5
  11.1 1.2 copy.17
  12.4 0.8 broadcast_bitcast_fusion.11
  13.1 0.7 convert_bitcast_fusion.1
  13.8 0.7 convert_bitcast_fusion
  14.5 1.0 dynamic-slice_multiply_fusion.1
  15.6 0.7 compare_select_fusion
  16.3 4.1 %copy.26 = bf16[256,4096]{0,1:T(8,128)(2,1)} copy(bf16[256,4096]{1,0:T(8,128)(2,1)} %param.9) | data formatting | bytes 4194304 | tf_op args[0]
  20.8 1.0 fusion.67
  21.9 1.0 fusion.61
  22.8 14.4 %collective-permute-done.7 = bf16[2,8]{1,0:T(2,128)(2,1)S(1)} collective-permute-done((bf16[2,8]{1,0:T(2,128)(2,1)S(1)}, bf16[2,8]{1,0:T(2,128)(2,1)S(1)}, u32[]{:S(2)}, u32[]{:S(2)}) %collective-permute-start.7) | collective-permute-done | bytes 64 | tf_op jit(solution)/shard_map/ppermute | solution.py:16
  37.3 10.6 %collective-permute-done.1 = bf16[2,8]{1,0:T(2,128)(2,1)S(1)} collective-permute-done((bf16[2,8]{1,0:T(2,128)(2,1)S(1)}, bf16[2,8]{1,0:T(2,128)(2,1)S(1)}, u32[]{:S(2)}, u32[]{:S(2)}) %collective-permute-start.1) | collective-permute-done | bytes 64 | tf_op jit(solution)/shard_map/ppermute | solution.py:16
  48.0 6.7 %collective-permute-start.9 = (bf16[2,8]{1,0:T(2,128)(2,1)S(1)}, bf16[2,8]{1,0:T(2,128)(2,1)S(1)}, u32[]{:S(2)}, u32[]{:S(2)}) collective-permute-start(bf16[2,8]{1,0:T(2,128)(2,1)S(1)} %collective-permute-done.7), channel_id=1, source_target_pairs={{0,1},{1,2},{2,3},{3,4},{4,5},{5,6},{6,7},{7,8},{8,9},{9,10},{10,1... | collective-permute-start | bytes 104 | tf_op jit(solution)/shard_map/ppermute | solution.py:16
  54.8 1.2 collective-permute-done.9
  56.1 2.1 collective-permute-done.3
  58.4 2.9 %collective-permute-done.11 = bf16[3,2,8]{2,1,0:T(2,128)(2,1)S(1)} collective-permute-done((bf16[3,2,8]{2,1,0:T(2,128)(2,1)S(1)}, bf16[3,2,8]{2,1,0:T(2,128)(2,1)S(1)}, u32[]{:S(2)}, u32[]{:S(2)}) %collective-permute-start.11) | collective-permute-done | bytes 128 | tf_op jit(solution)/shard_map/ppermute | solution.py:16
  61.2 6.5 %collective-permute-start.2 = (bf16[256,1024]{1,0:T(8,128)(2,1)S(1)}, bf16[256,1024]{1,0:T(8,128)(2,1)S(1)}, u32[]{:S(2)}, u32[]{:S(2)}) collective-permute-start(bf16[256,1024]{1,0:T(8,128)(2,1)S(1)} %collective-permute-done), channel_id=1, source_target_pairs={{0,1},{1,2},{2,3},{3,4},{4,5},{5,6},{6,7},{7,8},{8,9},{9,10},{10,1... | collective-permute-start | bytes 1572872 | tf_op jit(solution)/shard_map/ppermute | solution.py:16
  68.0 17.5 %collective-permute-done.2 = bf16[256,1024]{1,0:T(8,128)(2,1)S(1)} collective-permute-done((bf16[256,1024]{1,0:T(8,128)(2,1)S(1)}, bf16[256,1024]{1,0:T(8,128)(2,1)S(1)}, u32[]{:S(2)}, u32[]{:S(2)}) %collective-permute-start.2) | collective-permute-done | bytes 524320 | tf_op jit(solution)/shard_map/ppermute | solution.py:16
  85.5 1.3 pad_maximum_fusion
  86.8 10.7 %collective-permute-done.8 = bf16[256,1024]{0,1:T(8,128)(2,1)S(1)} collective-permute-done((bf16[256,1024]{0,1:T(8,128)(2,1)S(1)}, bf16[256,1024]{0,1:T(8,128)(2,1)S(1)}, u32[]{:S(2)}, u32[]{:S(2)}) %collective-permute-start.8) | collective-permute-done | bytes 524320 | tf_op jit(solution)/shard_map/ppermute | solution.py:16
  97.5 1.3 pad_maximum_fusion.1
  99.2 1.1 fusion.68
  100.3 1.0 fusion.62
  101.6 1.1 fusion.69
  102.7 28.0 %collective-permute-done.4 = bf16[3,256,1024]{2,1,0:T(8,128)(2,1)} collective-permute-done((bf16[3,256,1024]{2,1,0:T(8,128)(2,1)}, bf16[3,256,1024]{2,1,0:T(8,128)(2,1)}, u32[]{:S(2)}, u32[]{:S(2)}) %collective-permute-start.4) | collective-permute-done | bytes 1572896 | tf_op jit(solution)/shard_map/ppermute | solution.py:16
  130.7 2.7 %slice_convert_fusion = (f32[1,256,1024]{2,1,0:T(8,128)}, f32[1,256,1024]{2,1,0:T(8,128)S(1)}, f32[1,256,1024]{2,1,0:T(8,128)S(1)}) fusion(bf16[3,256,1024]{2,1,0:T(8,128)(2,1)} %collective-permute-done.4), kind=kLoop, calls=%fused_computation.71 | loop fusion | flops 786432 | bytes 4718592 | tf_op jit(solution)/shard_map/convert_element_type | solution.py:25
  133.4 1.3 copy.20
  134.8 0.3 copy.21
  135.1 1.6 copy.22
  136.7 10.9 %collective-permute-done.10 = bf16[3,256,1024]{1,2,0:T(8,128)(2,1)} collective-permute-done((bf16[3,256,1024]{1,2,0:T(8,128)(2,1)}, bf16[3,256,1024]{1,2,0:T(8,128)(2,1)}, u32[]{:S(2)}, u32[]{:S(2)}) %collective-permute-start.10) | collective-permute-done | bytes 1572896 | tf_op jit(solution)/shard_map/ppermute | solution.py:16
  147.6 1.5 fusion.78
  149.0 1.6 fusion.63
  150.7 1.1 fusion.64
  151.7 1.0 fusion.65
  152.8 1.1 fusion.66
  153.9 1.1 fusion.71
  155.0 1.1 fusion.72
  156.1 74.8 %while.11 = (s32[]{:T(128)}, bf16[8,256,4,128]{1,3,2,0:T(8,128)(2,1)}, bf16[8,1536,128]{1,2,0:T(8,128)(2,1)}, bf16[8,1536,128]{1,2,0:T(8,128)(2,1)}, bf16[8,256,...) while((s32[]{:T(128)}, bf16[8,256,4,128]{1,3,2,0:T(8,128)(2,1)}, ...), condition=%wide.region_3.4_spmd.clone, body=%wide.region_0.3_spmd.clone.sunk | while | flops 815400448 | bytes 8799317 | solution.py:99
  156.1 0.3 compare_bitcast_fusion.2
  156.4 5.8 %fusion.90 = (f32[4,256]{1,0:T(4,128)S(1)}, bf16[4,256,1536]{1,2,0:T(8,128)(2,1)}) fusion(pred[256,1536]{0,1:T(8,128)(4,1)S(1)} %compare_bitcast_fusion.2, bf16[8,1536,128]{1,2,0:T(8,128)(2,1)} %get-tuple-element.172, s32[]{:T(128)} %get-tuple-element.161, bf16[8,256,4,128]{1,3,2,0:T(8,128)(2,1)} %get-tuple-element.173), kind=kOutput, calls=%fused_computation.111.clone.1 | convolution fusion | flops 412091904 | bytes 4592640 | tf_op jit(solution)/shard_map/while/body/eval_jaxpr/sub | solution.py:93
  162.1 3.3 %fusion.91 = bf16[8,256,4,128]{1,3,2,0:T(8,128)(2,1)} fusion(bf16[8,256,4,128]{1,3,2,0:T(8,128)(2,1)} %get-tuple-element.162, s32[]{:T(128)} %get-tuple-element.161, bf16[4,256,1536]{1,2,0:T(8,128)(2,1)} %get-tuple-element.151, bf16[8,1536,128]{1,2,0:T(8,128)(2,1)} %get-tuple-element.171, f32[256,4]{0,1:T(4,128)S(1)} %bitcast.188), kind=kOutput, calls=%fused_computation.15.clone.1 | convolution fusion | flops 402915328 | bytes 3806208 | tf_op jit(solution)/shard_map/while/body/eval_jaxpr/gtc,cd->tgd/dot_general | solution.py:96
  165.4 0.3 compare_bitcast_fusion.2
  165.7 5.8 %fusion.90 = (f32[4,256]{1,0:T(4,128)S(1)}, bf16[4,256,1536]{1,2,0:T(8,128)(2,1)}) fusion(pred[256,1536]{0,1:T(8,128)(4,1)S(1)} %compare_bitcast_fusion.2, bf16[8,1536,128]{1,2,0:T(8,128)(2,1)} %get-tuple-element.172, s32[]{:T(128)} %get-tuple-element.161, bf16[8,256,4,128]{1,3,2,0:T(8,128)(2,1)} %get-tuple-element.173), kind=kOutput, calls=%fused_computation.111.clone.1 | convolution fusion | flops 412091904 | bytes 4592640 | tf_op jit(solution)/shard_map/while/body/eval_jaxpr/sub | solution.py:93
  171.5 3.3 %fusion.91 = bf16[8,256,4,128]{1,3,2,0:T(8,128)(2,1)} fusion(bf16[8,256,4,128]{1,3,2,0:T(8,128)(2,1)} %get-tuple-element.162, s32[]{:T(128)} %get-tuple-element.161, bf16[4,256,1536]{1,2,0:T(8,128)(2,1)} %get-tuple-element.151, bf16[8,1536,128]{1,2,0:T(8,128)(2,1)} %get-tuple-element.171, f32[256,4]{0,1:T(4,128)S(1)} %bitcast.188), kind=kOutput, calls=%fused_computation.15.clone.1 | convolution fusion | flops 402915328 | bytes 3806208 | tf_op jit(solution)/shard_map/while/body/eval_jaxpr/gtc,cd->tgd/dot_general | solution.py:96
  175.1 5.8 %fusion.90 = (f32[4,256]{1,0:T(4,128)S(1)}, bf16[4,256,1536]{1,2,0:T(8,128)(2,1)}) fusion(pred[256,1536]{0,1:T(8,128)(4,1)S(1)} %compare_bitcast_fusion.2, bf16[8,1536,128]{1,2,0:T(8,128)(2,1)} %get-tuple-element.172, s32[]{:T(128)} %get-tuple-element.161, bf16[8,256,4,128]{1,3,2,0:T(8,128)(2,1)} %get-tuple-element.173), kind=kOutput, calls=%fused_computation.111.clone.1 | convolution fusion | flops 412091904 | bytes 4592640 | tf_op jit(solution)/shard_map/while/body/eval_jaxpr/sub | solution.py:93
  180.8 3.3 %fusion.91 = bf16[8,256,4,128]{1,3,2,0:T(8,128)(2,1)} fusion(bf16[8,256,4,128]{1,3,2,0:T(8,128)(2,1)} %get-tuple-element.162, s32[]{:T(128)} %get-tuple-element.161, bf16[4,256,1536]{1,2,0:T(8,128)(2,1)} %get-tuple-element.151, bf16[8,1536,128]{1,2,0:T(8,128)(2,1)} %get-tuple-element.171, f32[256,4]{0,1:T(4,128)S(1)} %bitcast.188), kind=kOutput, calls=%fused_computation.15.clone.1 | convolution fusion | flops 402915328 | bytes 3806208 | tf_op jit(solution)/shard_map/while/body/eval_jaxpr/gtc,cd->tgd/dot_general | solution.py:96
  184.4 5.8 %fusion.90 = (f32[4,256]{1,0:T(4,128)S(1)}, bf16[4,256,1536]{1,2,0:T(8,128)(2,1)}) fusion(pred[256,1536]{0,1:T(8,128)(4,1)S(1)} %compare_bitcast_fusion.2, bf16[8,1536,128]{1,2,0:T(8,128)(2,1)} %get-tuple-element.172, s32[]{:T(128)} %get-tuple-element.161, bf16[8,256,4,128]{1,3,2,0:T(8,128)(2,1)} %get-tuple-element.173), kind=kOutput, calls=%fused_computation.111.clone.1 | convolution fusion | flops 412091904 | bytes 4592640 | tf_op jit(solution)/shard_map/while/body/eval_jaxpr/sub | solution.py:93
  190.2 3.3 %fusion.91 = bf16[8,256,4,128]{1,3,2,0:T(8,128)(2,1)} fusion(bf16[8,256,4,128]{1,3,2,0:T(8,128)(2,1)} %get-tuple-element.162, s32[]{:T(128)} %get-tuple-element.161, bf16[4,256,1536]{1,2,0:T(8,128)(2,1)} %get-tuple-element.151, bf16[8,1536,128]{1,2,0:T(8,128)(2,1)} %get-tuple-element.171, f32[256,4]{0,1:T(4,128)S(1)} %bitcast.188), kind=kOutput, calls=%fused_computation.15.clone.1 | convolution fusion | flops 402915328 | bytes 3806208 | tf_op jit(solution)/shard_map/while/body/eval_jaxpr/gtc,cd->tgd/dot_general | solution.py:96
  193.8 5.8 %fusion.90 = (f32[4,256]{1,0:T(4,128)S(1)}, bf16[4,256,1536]{1,2,0:T(8,128)(2,1)}) fusion(pred[256,1536]{0,1:T(8,128)(4,1)S(1)} %compare_bitcast_fusion.2, bf16[8,1536,128]{1,2,0:T(8,128)(2,1)} %get-tuple-element.172, s32[]{:T(128)} %get-tuple-element.161, bf16[8,256,4,128]{1,3,2,0:T(8,128)(2,1)} %get-tuple-element.173), kind=kOutput, calls=%fused_computation.111.clone.1 | convolution fusion | flops 412091904 | bytes 4592640 | tf_op jit(solution)/shard_map/while/body/eval_jaxpr/sub | solution.py:93
  199.5 3.3 %fusion.91 = bf16[8,256,4,128]{1,3,2,0:T(8,128)(2,1)} fusion(bf16[8,256,4,128]{1,3,2,0:T(8,128)(2,1)} %get-tuple-element.162, s32[]{:T(128)} %get-tuple-element.161, bf16[4,256,1536]{1,2,0:T(8,128)(2,1)} %get-tuple-element.151, bf16[8,1536,128]{1,2,0:T(8,128)(2,1)} %get-tuple-element.171, f32[256,4]{0,1:T(4,128)S(1)} %bitcast.188), kind=kOutput, calls=%fused_computation.15.clone.1 | convolution fusion | flops 402915328 | bytes 3806208 | tf_op jit(solution)/shard_map/while/body/eval_jaxpr/gtc,cd->tgd/dot_general | solution.py:96
  203.1 5.8 %fusion.90 = (f32[4,256]{1,0:T(4,128)S(1)}, bf16[4,256,1536]{1,2,0:T(8,128)(2,1)}) fusion(pred[256,1536]{0,1:T(8,128)(4,1)S(1)} %compare_bitcast_fusion.2, bf16[8,1536,128]{1,2,0:T(8,128)(2,1)} %get-tuple-element.172, s32[]{:T(128)} %get-tuple-element.161, bf16[8,256,4,128]{1,3,2,0:T(8,128)(2,1)} %get-tuple-element.173), kind=kOutput, calls=%fused_computation.111.clone.1 | convolution fusion | flops 412091904 | bytes 4592640 | tf_op jit(solution)/shard_map/while/body/eval_jaxpr/sub | solution.py:93
  208.9 3.3 %fusion.91 = bf16[8,256,4,128]{1,3,2,0:T(8,128)(2,1)} fusion(bf16[8,256,4,128]{1,3,2,0:T(8,128)(2,1)} %get-tuple-element.162, s32[]{:T(128)} %get-tuple-element.161, bf16[4,256,1536]{1,2,0:T(8,128)(2,1)} %get-tuple-element.151, bf16[8,1536,128]{1,2,0:T(8,128)(2,1)} %get-tuple-element.171, f32[256,4]{0,1:T(4,128)S(1)} %bitcast.188), kind=kOutput, calls=%fused_computation.15.clone.1 | convolution fusion | flops 402915328 | bytes 3806208 | tf_op jit(solution)/shard_map/while/body/eval_jaxpr/gtc,cd->tgd/dot_general | solution.py:96
  212.5 5.8 %fusion.90 = (f32[4,256]{1,0:T(4,128)S(1)}, bf16[4,256,1536]{1,2,0:T(8,128)(2,1)}) fusion(pred[256,1536]{0,1:T(8,128)(4,1)S(1)} %compare_bitcast_fusion.2, bf16[8,1536,128]{1,2,0:T(8,128)(2,1)} %get-tuple-element.172, s32[]{:T(128)} %get-tuple-element.161, bf16[8,256,4,128]{1,3,2,0:T(8,128)(2,1)} %get-tuple-element.173), kind=kOutput, calls=%fused_computation.111.clone.1 | convolution fusion | flops 412091904 | bytes 4592640 | tf_op jit(solution)/shard_map/while/body/eval_jaxpr/sub | solution.py:93
  218.2 3.3 %fusion.91 = bf16[8,256,4,128]{1,3,2,0:T(8,128)(2,1)} fusion(bf16[8,256,4,128]{1,3,2,0:T(8,128)(2,1)} %get-tuple-element.162, s32[]{:T(128)} %get-tuple-element.161, bf16[4,256,1536]{1,2,0:T(8,128)(2,1)} %get-tuple-element.151, bf16[8,1536,128]{1,2,0:T(8,128)(2,1)} %get-tuple-element.171, f32[256,4]{0,1:T(4,128)S(1)} %bitcast.188), kind=kOutput, calls=%fused_computation.15.clone.1 | convolution fusion | flops 402915328 | bytes 3806208 | tf_op jit(solution)/shard_map/while/body/eval_jaxpr/gtc,cd->tgd/dot_general | solution.py:96
  221.8 5.8 %fusion.90 = (f32[4,256]{1,0:T(4,128)S(1)}, bf16[4,256,1536]{1,2,0:T(8,128)(2,1)}) fusion(pred[256,1536]{0,1:T(8,128)(4,1)S(1)} %compare_bitcast_fusion.2, bf16[8,1536,128]{1,2,0:T(8,128)(2,1)} %get-tuple-element.172, s32[]{:T(128)} %get-tuple-element.161, bf16[8,256,4,128]{1,3,2,0:T(8,128)(2,1)} %get-tuple-element.173), kind=kOutput, calls=%fused_computation.111.clone.1 | convolution fusion | flops 412091904 | bytes 4592640 | tf_op jit(solution)/shard_map/while/body/eval_jaxpr/sub | solution.py:93
  227.6 3.3 %fusion.91 = bf16[8,256,4,128]{1,3,2,0:T(8,128)(2,1)} fusion(bf16[8,256,4,128]{1,3,2,0:T(8,128)(2,1)} %get-tuple-element.162, s32[]{:T(128)} %get-tuple-element.161, bf16[4,256,1536]{1,2,0:T(8,128)(2,1)} %get-tuple-element.151, bf16[8,1536,128]{1,2,0:T(8,128)(2,1)} %get-tuple-element.171, f32[256,4]{0,1:T(4,128)S(1)} %bitcast.188), kind=kOutput, calls=%fused_computation.15.clone.1 | convolution fusion | flops 402915328 | bytes 3806208 | tf_op jit(solution)/shard_map/while/body/eval_jaxpr/gtc,cd->tgd/dot_general | solution.py:96
  230.9 4.1 %copy.31 = bf16[256,4096]{1,0:T(8,128)(2,1)} copy(bf16[256,4096]{0,1:T(8,128)(2,1)} %bitcast.170) | data formatting | bytes 4194304 | tf_op jit(solution)/shard_map/reshape | solution.py:100
  (54 shorter events, 3.6 us)
Async XLA Ops:
  1.2 66.6 %collective-permute-start.6 = (bf16[256,1024]{0,1:T(8,128)(2,1)S(1)}, bf16[256,1024]{0,1:T(8,128)(2,1)S(1)}, u32[]{:S(2)}, u32[]{:S(2)}) collective-permute-start(bf16[256,1024]{0,1:T(8,128)(2,1)S(1)} %copy.23), channel_id=1, source_target_pairs={{0,1},{1,2},{2,3},{3,4},{4,5},{5,6},{6,7},{7,8},{8,9},{9,10},{10,1... | collective-permute-start | bytes 1572872 | tf_op jit(solution)/shard_map/ppermute | solution.py:16
  5.5 31.7 %collective-permute-start.7 = (bf16[2,8]{1,0:T(2,128)(2,1)S(1)}, bf16[2,8]{1,0:T(2,128)(2,1)S(1)}, u32[]{:S(2)}, u32[]{:S(2)}) collective-permute-start(bf16[2,8]{1,0:T(2,128)(2,1)S(1)} %convert_element_type.193), channel_id=1, source_target_pairs={{0,1},{1,2},{2,3},{3,4},{4,5},{5,6},{6,7},{7,8},{8,9},{9,10},{10,1... | collective-permute-start | bytes 104 | tf_op jit(solution)/shard_map/ppermute | solution.py:16
  7.0 54.2 %collective-permute-start = (bf16[256,1024]{1,0:T(8,128)(2,1)}, bf16[256,1024]{1,0:T(8,128)(2,1)S(1)}, u32[]{:S(2)}, u32[]{:S(2)}) collective-permute-start(bf16[256,1024]{1,0:T(8,128)(2,1)} %param.11), channel_id=1, source_target_pairs={{0,1},{1,2},{2,3},{3,4},{4,5},{5,6},{6,7},{7,8},{8,9},{9,10},{10,1... | collective-permute-start | bytes 1572872 | tf_op jit(solution)/shard_map/ppermute | solution.py:16
  9.2 38.8 %collective-permute-start.1 = (bf16[2,8]{1,0:T(2,128)(2,1)S(1)}, bf16[2,8]{1,0:T(2,128)(2,1)S(1)}, u32[]{:S(2)}, u32[]{:S(2)}) collective-permute-start(bf16[2,8]{1,0:T(2,128)(2,1)S(1)} %convert_element_type.171), channel_id=1, source_target_pairs={{0,1},{1,2},{2,3},{3,4},{4,5},{5,6},{6,7},{7,8},{8,9},{9,10},{10,1... | collective-permute-start | bytes 104 | tf_op jit(solution)/shard_map/ppermute | solution.py:16
  16.3 69.2 %copy-start.1 = (bf16[256,1024]{1,0:T(8,128)(2,1)S(1)}, bf16[256,1024]{1,0:T(8,128)(2,1)}, u32[]{:S(2)}) copy-start(bf16[256,1024]{1,0:T(8,128)(2,1)} %param.11) | copy-start | bytes 1572868
  48.0 8.0 %collective-permute-start.9 = (bf16[2,8]{1,0:T(2,128)(2,1)S(1)}, bf16[2,8]{1,0:T(2,128)(2,1)S(1)}, u32[]{:S(2)}, u32[]{:S(2)}) collective-permute-start(bf16[2,8]{1,0:T(2,128)(2,1)S(1)} %collective-permute-done.7), channel_id=1, source_target_pairs={{0,1},{1,2},{2,3},{3,4},{4,5},{5,6},{6,7},{7,8},{8,9},{9,10},{10,1... | collective-permute-start | bytes 104 | tf_op jit(solution)/shard_map/ppermute | solution.py:16
  54.7 3.5 %collective-permute-start.3 = (bf16[2,8]{1,0:T(2,128)(2,1)S(1)}, bf16[2,8]{1,0:T(2,128)(2,1)S(1)}, u32[]{:S(2)}, u32[]{:S(2)}) collective-permute-start(bf16[2,8]{1,0:T(2,128)(2,1)S(1)} %collective-permute-done.1), channel_id=1, source_target_pairs={{0,1},{1,2},{2,3},{3,4},{4,5},{5,6},{6,7},{7,8},{8,9},{9,10},{10,1... | collective-permute-start | bytes 104 | tf_op jit(solution)/shard_map/ppermute | solution.py:16
  56.1 5.2 %collective-permute-start.11 = (bf16[3,2,8]{2,1,0:T(2,128)(2,1)S(1)}, bf16[3,2,8]{2,1,0:T(2,128)(2,1)S(1)}, u32[]{:S(2)}, u32[]{:S(2)}) collective-permute-start(bf16[3,2,8]{2,1,0:T(2,128)(2,1)S(1)} %pad_maximum_fusion.3), channel_id=1, source_target_pairs={{0,16},{16,32},{32,48},{48,64},{64,80},{80,96},{96,112},{112,128},... | collective-permute-start | bytes 296 | tf_op jit(solution)/shard_map/ppermute | solution.py:16
  58.3 9.6 %collective-permute-start.5 = (bf16[3,2,8]{2,1,0:T(2,128)(2,1)S(1)}, bf16[3,2,8]{2,1,0:T(2,128)(2,1)S(1)}, u32[]{:S(2)}, u32[]{:S(2)}) collective-permute-start(bf16[3,2,8]{2,1,0:T(2,128)(2,1)S(1)} %pad_maximum_fusion.2), channel_id=1, source_target_pairs={{0,16},{16,32},{32,48},{48,64},{64,80},{80,96},{96,112},{112,128},... | collective-permute-start | bytes 296 | tf_op jit(solution)/shard_map/ppermute | solution.py:16
  61.2 24.3 %collective-permute-start.2 = (bf16[256,1024]{1,0:T(8,128)(2,1)S(1)}, bf16[256,1024]{1,0:T(8,128)(2,1)S(1)}, u32[]{:S(2)}, u32[]{:S(2)}) collective-permute-start(bf16[256,1024]{1,0:T(8,128)(2,1)S(1)} %collective-permute-done), channel_id=1, source_target_pairs={{0,1},{1,2},{2,3},{3,4},{4,5},{5,6},{6,7},{7,8},{8,9},{9,10},{10,1... | collective-permute-start | bytes 1572872 | tf_op jit(solution)/shard_map/ppermute | solution.py:16
  67.9 29.6 %collective-permute-start.8 = (bf16[256,1024]{0,1:T(8,128)(2,1)S(1)}, bf16[256,1024]{0,1:T(8,128)(2,1)S(1)}, u32[]{:S(2)}, u32[]{:S(2)}) collective-permute-start(bf16[256,1024]{0,1:T(8,128)(2,1)S(1)} %collective-permute-done.6), channel_id=1, source_target_pairs={{0,1},{1,2},{2,3},{3,4},{4,5},{5,6},{6,7},{7,8},{8,9},{9,10},{10,1... | collective-permute-start | bytes 1572872 | tf_op jit(solution)/shard_map/ppermute | solution.py:16
  86.8 43.9 %collective-permute-start.4 = (bf16[3,256,1024]{2,1,0:T(8,128)(2,1)}, bf16[3,256,1024]{2,1,0:T(8,128)(2,1)}, u32[]{:S(2)}, u32[]{:S(2)}) collective-permute-start(bf16[3,256,1024]{2,1,0:T(8,128)(2,1)} %pad_maximum_fusion), channel_id=1, source_target_pairs={{0,16},{16,32},{32,48},{48,64},{64,80},{80,96},{96,112},{112,128},... | collective-permute-start | bytes 4718600 | tf_op jit(solution)/shard_map/ppermute | solution.py:16
  97.5 1.5 copy-start.2
  98.8 48.8 %collective-permute-start.10 = (bf16[3,256,1024]{1,2,0:T(8,128)(2,1)}, bf16[3,256,1024]{1,2,0:T(8,128)(2,1)}, u32[]{:S(2)}, u32[]{:S(2)}) collective-permute-start(bf16[3,256,1024]{1,2,0:T(8,128)(2,1)} %pad_maximum_fusion.1), channel_id=1, source_target_pairs={{0,16},{16,32},{32,48},{48,64},{64,80},{80,96},{96,112},{112,128},... | collective-permute-start | bytes 4718600 | tf_op jit(solution)/shard_map/ppermute | solution.py:16
  99.0 2.6 %copy-start.3 = (bf16[256,1024]{0,1:T(8,128)(2,1)S(1)}, bf16[256,1024]{0,1:T(8,128)(2,1)}, u32[]{:S(2)}) copy-start(bf16[256,1024]{0,1:T(8,128)(2,1)} %copy-done.2) | copy-start | bytes 1572868
  136.7 14.0 %copy-start = (f32[1,256,1024]{1,2,0:T(8,128)S(1)}, f32[1,256,1024]{1,2,0:T(8,128)}, u32[]{:S(2)}) copy-start(f32[1,256,1024]{1,2,0:T(8,128)} %copy.20) | copy-start | bytes 3145732
where the time goes:
time: 236 us; the launch traced here: 235 us
  waiting for transfers between devices  98.2 us (42%)
  matrix products  72.6 us (31%)
  other arithmetic  24.8 us (11%)
  starting transfers between devices  21.3 us (9%)
  local copies, waits for them, and re-layouts  17.9 us (8%)
    ppermute x12, waiting for transfers between devices, from_behind(): lax.ppermute(array, axis, [(i, (i + by) % count) for i in range(count)])  98.2 us
    sub x8, matrix products, one_head(): expo = jnp.where(allowed, jnp.exp(masked - peak), 0.0)  46.1 us
    dot_general x8, matrix products, one_head(): jnp.einsum('gtc,cd->tgd', weights, vhead, preferred_element_type=jnp.floa...  26.5 us
    ppermute x12, starting transfers between devices, from_behind(): lax.ppermute(array, axis, [(i, (i + by) % count) for i in range(count)])  21.3 us
    unnamed x15, other arithmetic  10.5 us
    unnamed x10, local copies, waits for them, and re-layouts  5.38 us
    convert_element_type x6, local copies, waits for them, and re-layouts, dequantize(): code_matrix.reshape(2, block_rows // 2, KEY_HEADS, HEAD_SIZE)  4.88 us
  transfers between devices with their start and end apart: 12, of which 9 were waited for; matrix products, arithmetic and copies ran while one was open for 11% of the time, Pallas kernels for 0%

commit v1 on v0

v1 whole, which is shorter than its diff:
```python
import math

import jax
import jax.numpy as jnp
from jax import lax
from jax.experimental import pallas as pl
from jax.experimental.pallas import tpu as pltpu
from jax.sharding import PartitionSpec as P

MESH = pl.DeviceIdType.MESH
KEY_HEADS = 8
GROUP = 4
SIZE = 128
SPAN = 128
ROWS = 256
SLOTS = 6
EXP_SCALE = math.log2(math.e) / math.sqrt(SIZE)

OWN, IN1, IN2, OUT0, OUT1, OUT2, VIA_Z, VIA_X, VIA_Y = range(9)
F_IN1, F_DOWN, F_OUT0, F_WRAP, F_DOWN2, F_UP2, F_OUT1, F_OUT2, F_YWRAP = range(9)

UP_HEADS = 3
FIRST_HEADS = (5, 6)
AHEAD = 1
LEADS = (0, 1, 1, 2, 3, 4, 5)


def kernel(
    kscale, vscale, formats, order, k_ref, v_ref, q_hbm, out_hbm,
    kv, bias, q_ref, o_ref, recv, sent, q_sem, o_sem,
):
    o = lax.axis_index("outer")
    i = lax.axis_index("inner")
    c = o % 2
    y = (o // 2) % 4
    x = i % 4
    zh = i // 4

    def swapped(h):
        return (h * 3) % KEY_HEADS

    def up(h):
        return swapped(h) < UP_HEADS

    def x_first(h):
        return swapped(h) < jnp.where(c == 0, FIRST_HEADS[0], FIRST_HEADS[1])

    next_in = (i + 1) % 16
    next_out = (o + 1) % 16
    source_x = (x + 1) % 4
    down_to = zh * 4 + (x + 3) % 4
    down2_to = (zh * 4 + source_x + 2) % 16
    wraps_y = o == 7

    q_copy = pltpu.make_async_copy(q_hbm, q_ref, q_sem)
    q_copy.start()

    barrier = pltpu.get_barrier_semaphore()

    def greet(outer, inner):
        pl.semaphore_signal(barrier, inc=1, device_id=(outer, inner), device_id_type=MESH)

    greet(o, (i + 15) % 16)
    greet(o, zh * 4 + (x + 1) % 4)
    two_back = (i + 14) % 16
    greet(o, (two_back // 4) * 4 + (x + 1) % 4)
    greet((o + 15) % 16, i)

    @pl.when(x == 0)
    def _():
        greet(o, i + 3)
        greet(o, (i + 12) % 16)

    @pl.when(jnp.logical_or(o == 1, o == 3))
    def _():
        greet(7, i)

    @pl.when(o == 8)
    def _():
        greet(1, i)
        greet(3, i)

    for h in range(KEY_HEADS):
        for which, codes, scale in ((0, k_ref, kscale), (1, v_ref, vscale)):
            unit = jnp.where(formats[which, h] == 0, 1.0, 0.25)
            for s in range(2):
                rows = pl.ds(s * SPAN, SPAN)
                part = codes[rows, h * SIZE:(h + 1) * SIZE].astype(jnp.float32)
                kv[h, OWN, which, rows] = (part * (scale[s, h] * unit)).astype(jnp.bfloat16)

    peers = (
        4
        + jnp.where(jnp.logical_or(x == 0, x == 3), 1, 0)
        + jnp.where(jnp.logical_or(o == 1, o == 3), 1, 0)
        + jnp.where(wraps_y, 2, 0)
    )
    pl.semaphore_wait(barrier, peers)

    def send(h, source, target, flow, device):
        pltpu.make_async_remote_copy(
            kv.at[h, source], kv.at[h, target], sent.at[h, flow], recv.at[h, target],
            device_id=device, device_id_type=MESH,
        ).start()

    def arrived(h, slot):
        pltpu.make_async_copy(kv.at[h, slot], kv.at[h, slot], recv.at[h, slot]).wait()

    def left(h, flow):
        pltpu.make_async_copy(kv.at[h, OWN], kv.at[h, OWN], sent.at[h, flow]).wait()

    def send_own(h):
        round_x = jnp.logical_and(x == 3, x_first(h))

        @pl.when(round_x)
        def _():
            send(h, OWN, VIA_Z, F_IN1, (o, i - 3))

        @pl.when(jnp.logical_not(round_x))
        def _():
            send(h, OWN, IN1, F_IN1, (o, next_in))

        @pl.when(jnp.logical_not(up(h)))
        def _():
            send(h, OWN, VIA_X, F_DOWN, (o, down_to))

        send(h, OWN, OUT0, F_OUT0, (next_out, i))

    def relay_wrap(h):
        @pl.when(jnp.logical_and(x == 0, x_first(h)))
        def _():
            arrived(h, VIA_Z)
            send(h, VIA_Z, IN1, F_WRAP, (o, (i + 4) % 16))

    def relay_down(h):
        @pl.when(jnp.logical_not(up(h)))
        def _():
            arrived(h, VIA_X)
            send(h, VIA_X, IN2, F_DOWN2, (o, down2_to))

    def relay_in1(h):
        arrived(h, IN1)

        @pl.when(up(h))
        def _():
            send(h, IN1, IN2, F_UP2, (o, next_in))

        @pl.when(wraps_y)
        def _():
            send(h, IN1, VIA_Y, F_OUT1, (1, i))

        @pl.when(jnp.logical_not(wraps_y))
        def _():
            send(h, IN1, OUT1, F_OUT1, (next_out, i))

    def relay_in2(h):
        arrived(h, IN2)

        @pl.when(wraps_y)
        def _():
            send(h, IN2, VIA_Y, F_OUT2, (3, i))

        @pl.when(jnp.logical_not(wraps_y))
        def _():
            send(h, IN2, OUT2, F_OUT2, (next_out, i))

    def relay_y(h):
        @pl.when(o == 1)
        def _():
            arrived(h, VIA_Y)
            send(h, VIA_Y, OUT1, F_YWRAP, (8, i))

        @pl.when(o == 3)
        def _():
            arrived(h, VIA_Y)
            send(h, VIA_Y, OUT2, F_YWRAP, (8, i))

    def out_copy(h):
        return pltpu.make_async_copy(
            o_ref.at[h],
            out_hbm.at[:, pl.ds(pl.multiple_of(h * (GROUP * SIZE), GROUP * SIZE), GROUP * SIZE)],
            o_sem.at[h],
        )

    def attend(h):
        arrived(h, OUT0)
        arrived(h, OUT1)
        arrived(h, OUT2)

        @pl.when(h == 0)
        def _():
            q_copy.wait()

        for g in range(GROUP):
            columns = pl.ds(pl.multiple_of((h * GROUP + g) * SIZE, SIZE), SIZE)
            keys = kv[h, 0:SLOTS, 0].reshape(SLOTS * ROWS, SIZE)
            values = kv[h, 0:SLOTS, 1].reshape(SLOTS * ROWS, SIZE)
            score = lax.dot_general(
                q_ref[:, columns], keys, (((1,), (1,)), ((), ())),
                preferred_element_type=jnp.float32,
            ) + bias[...]
            peak = jnp.max(score, axis=1, keepdims=True)
            expo = jnp.exp2((score - peak) * EXP_SCALE)
            total = jnp.sum(expo, axis=1, keepdims=True)
            summed = jnp.dot(expo.astype(jnp.bfloat16), values, preferred_element_type=jnp.float32)
            o_ref[h, :, g * SIZE:(g + 1) * SIZE] = (summed / total).astype(jnp.bfloat16)
        out_copy(h).start()

    stages = (send_own, relay_wrap, relay_down, relay_in1, relay_in2, relay_y, attend)

    def first(h, carry):
        send_own(h)
        return carry

    def step(t, carry):
        for stage, lead in zip(stages, LEADS):
            h = t - lead + (AHEAD if stage is send_own else 0)

            @pl.when(jnp.logical_and(h >= 0, h < KEY_HEADS))
            def _():
                stage(h)

        return carry

    lax.fori_loop(0, AHEAD, first, 0)

    below = lax.broadcasted_iota(jnp.int32, (SPAN, SPAN), 0)
    across = lax.broadcasted_iota(jnp.int32, (SPAN, SPAN), 1)
    for slot, (d_out, d_in) in enumerate(((0, 0), (0, 1), (0, 2), (1, 0), (1, 1), (1, 2))):
        block = ((o + 16 - d_out) % 16) * 16 + (i + 16 - d_in) % 16
        for s in range(2):
            key_at = order[block * 2 + s] * SPAN
            for r in range(2):
                query_at = order[(o * 16 + i) * 2 + r] * SPAN
                seen = key_at + across <= query_at + below
                bias[r * SPAN:(r + 1) * SPAN, (slot * 2 + s) * SPAN:(slot * 2 + s + 1) * SPAN] = (
                    jnp.where(seen, 0.0, -jnp.inf)
                )

    lax.fori_loop(0, KEY_HEADS + LEADS[-1], step, 0)

    def finish(h, carry):
        out_copy(h).wait()
        for flow in (F_IN1, F_OUT0, F_OUT1, F_OUT2):
            left(h, flow)

        @pl.when(up(h))
        def _():
            left(h, F_UP2)

        @pl.when(jnp.logical_not(up(h)))
        def _():
            left(h, F_DOWN)
            left(h, F_DOWN2)

        @pl.when(jnp.logical_and(x == 0, x_first(h)))
        def _():
            left(h, F_WRAP)

        @pl.when(jnp.logical_or(o == 1, o == 3))
        def _():
            left(h, F_YWRAP)

        return carry

    lax.fori_loop(0, KEY_HEADS, finish, 0)


def shards(queries, key_codes, value_code_rows, key_scales, value_scales, formats, span_order):
    vmem = pl.BlockSpec(memory_space=pltpu.VMEM)
    smem = pl.BlockSpec(memory_space=pltpu.SMEM)
    anywhere = pl.BlockSpec(memory_space=pl.ANY)
    flops = 4 * 32 * ROWS * SLOTS * ROWS * SIZE
    return pl.pallas_call(
        kernel,
        out_shape=jax.ShapeDtypeStruct((ROWS, KEY_HEADS * GROUP * SIZE), jnp.bfloat16),
        in_specs=[smem, smem, smem, smem, vmem, vmem, anywhere],
        out_specs=anywhere,
        scratch_shapes=[
            pltpu.VMEM((KEY_HEADS, 9, 2, ROWS, SIZE), jnp.bfloat16),
            pltpu.VMEM((ROWS, SLOTS * ROWS), jnp.float32),
            pltpu.VMEM((ROWS, KEY_HEADS * GROUP * SIZE), jnp.bfloat16),
            pltpu.VMEM((KEY_HEADS, ROWS, GROUP * SIZE), jnp.bfloat16),
            pltpu.SemaphoreType.DMA((KEY_HEADS, 9)),
            pltpu.SemaphoreType.DMA((KEY_HEADS, 9)),
            pltpu.SemaphoreType.DMA,
            pltpu.SemaphoreType.DMA((KEY_HEADS,)),
        ],
        compiler_params=pltpu.CompilerParams(
            collective_id=1, has_side_effects=True, vmem_limit_bytes=48 * 2**20
        ),
        cost_estimate=pl.CostEstimate(
            flops=flops, bytes_accessed=6 * 2**20, transcendentals=32 * ROWS * SLOTS * ROWS
        ),
        name="block_window_attention",
    )(key_scales, value_scales, formats, span_order, key_codes, value_code_rows, queries)


def solution(mesh):
    split = P(("outer", "inner"), None)
    return jax.shard_map(
        shards,
        mesh=mesh,
        in_specs=(split, split, split, split, split, P(), P()),
        out_specs=split,
        check_vma=False,
    )
```

time: 236 us -> 91.1 us (0.39)
  the two profiles are of different devices: /device:TPU:102 before, /device:TPU:34 now
where the time goes in v1:
time: 91.1 us; the launch traced here: 89.5 us
  Pallas kernels  81.8 us (90%)
  local copies, waits for them, and re-layouts  7.71 us (8%)
    pallas_call x1, Pallas kernels, shards(): pl.pallas_call(kernel, out_shape=jax.ShapeDtypeStruct((ROWS, KEY_HEADS *...  81.8 us
    unnamed x15, local copies, waits for them, and re-layouts  7.71 us

profile of v1, /device:TPU:34, one launch (start us, length us, event | category | flops | bytes accessed | tf_op | source)
XLA Modules:
  0.0 89.5 jit_solution(9913596428174095841)
XLA Ops:
  0.0 0.0 copy-start
  0.0 1.6 %copy-done = bf16[256,4096]{1,0:T(8,128)(2,1)S(1)} copy-done((bf16[256,4096]{1,0:T(8,128)(2,1)S(1)}, bf16[256,4096]{1,0:T(8,128)(2,1)}, u32[]{:S(2)}) %copy-start) | copy-done | bytes 2097176
  1.6 0.0 copy-start.1
  1.6 1.0 %copy-done.1 = bf16[256,1024]{1,0:T(8,128)(2,1)S(1)} copy-done((bf16[256,1024]{1,0:T(8,128)(2,1)S(1)}, bf16[256,1024]{1,0:T(8,128)(2,1)}, u32[]{:S(2)}) %copy-start.1) | copy-done | bytes 524312
  2.6 0.0 copy-start.2
  2.6 1.0 %copy-done.2 = bf16[256,1024]{1,0:T(8,128)(2,1)S(1)} copy-done((bf16[256,1024]{1,0:T(8,128)(2,1)S(1)}, bf16[256,1024]{1,0:T(8,128)(2,1)}, u32[]{:S(2)}) %copy-start.2) | copy-done | bytes 524312
  3.7 0.0 copy-start.3
  3.7 0.7 copy-done.3
  4.4 0.0 copy-start.4
  4.4 0.7 copy-done.4
  5.0 0.0 copy-start.5
  5.0 0.7 copy-done.5
  5.7 0.0 copy-start.6
  5.7 0.7 copy-done.6
  6.4 81.8 %block_window_attention.1 = bf16[256,4096]{1,0:T(8,128)(2,1)S(1)} custom-call(f32[2,8]{1,0:T(2,128)S(1)} %copy-done.4, f32[2,8]{1,0:T(2,128)S(1)} %copy-done.5, s32[2,8]{1,0:T(2,128)S(1)} %copy-done.6, s32[512]{0:T(512)S(1)} %copy-done.3, bf16[256,1024]{1,0:T(8,128)(2,1)S(1)} %copy-done.1, bf16[256,1024]{1,0:T(8,128)(2,1)S(1)} %copy-done.2, ...), custom_call_target="tpu_custom_call" | custom-call | flops 6442450944 | bytes 6291456 | tf_op jit(solution)/shard_map/block_window_attention/pallas_call | solution.py:273
  88.2 1.3 %copy.9 = bf16[256,4096]{1,0:T(8,128)(2,1)} copy(bf16[256,4096]{1,0:T(8,128)(2,1)S(1)} %block_window_attention.1) | data formatting | bytes 4194304
Async XLA Ops:
  0.0 1.6 %copy-start = (bf16[256,4096]{1,0:T(8,128)(2,1)S(1)}, bf16[256,4096]{1,0:T(8,128)(2,1)}, u32[]{:S(2)}) copy-start(bf16[256,4096]{1,0:T(8,128)(2,1)} %q_hbm.1) | copy-start | bytes 6291460
  1.6 1.0 %copy-start.1 = (bf16[256,1024]{1,0:T(8,128)(2,1)S(1)}, bf16[256,1024]{1,0:T(8,128)(2,1)}, u32[]{:S(2)}) copy-start(bf16[256,1024]{1,0:T(8,128)(2,1)} %k_ref.1) | copy-start | bytes 1572868
  2.6 1.0 %copy-start.2 = (bf16[256,1024]{1,0:T(8,128)(2,1)S(1)}, bf16[256,1024]{1,0:T(8,128)(2,1)}, u32[]{:S(2)}) copy-start(bf16[256,1024]{1,0:T(8,128)(2,1)} %v_ref.1) | copy-start | bytes 1572868
  3.7 0.7 copy-start.3
  4.4 0.7 copy-start.4
  5.0 0.7 copy-start.5
  5.7 0.7 copy-start.6

commit v2 on v1

v2 whole, which is shorter than its diff:
```python
import math

import jax
import jax.numpy as jnp
from jax import lax
from jax.experimental import pallas as pl
from jax.experimental.pallas import tpu as pltpu
from jax.sharding import PartitionSpec as P

MESH = pl.DeviceIdType.MESH
KEY_HEADS = 8
GROUP = 4
SIZE = 128
SPAN = 128
ROWS = 256
SLOTS = 6
HALF = 3
EXP_SCALE = math.log2(math.e) / math.sqrt(SIZE)

OWN, OUT0, IN1, IN2, OUT1, OUT2, VIA_Z, VIA_X, VIA_Y = range(9)
F_IN1, F_DOWN, F_OUT0, F_WRAP, F_DOWN2, F_UP2, F_OUT1, F_OUT2, F_YWRAP = range(9)

UP = (128, 256, 80, 352)
HIGH = 384
FIRST = 304
BOTH = 2 * ROWS


def plan_of(
    send_in, send_out, relay_wrap, relay_down, relay_in1, relay_in2, relay_y0, relay_y,
    attend_near, attend_far
):
    return (
        (send_in, -1),
        (relay_wrap, 1),
        (relay_y0, 1),
        (relay_down, 1),
        (relay_in1, 2),
        (relay_in2, 3),
        (relay_y, 3),
        (send_out, -1),
        (attend_near(range(GROUP)), 3),
        (attend_far(range(GROUP)), 4),
    )


def kernel(
    kscale, vscale, formats, order, k_hbm, v_hbm, q_hbm, out_hbm,
    kv, bias, sums, peaks, totals, k_ref, v_ref, q_ref, o_ref, recv, sent, in_sem, o_sem,
):
    o = lax.axis_index("outer")
    i = lax.axis_index("inner")
    c = o % 2
    y = (o // 2) % 4
    x = i % 4
    zh = i // 4

    next_in = (i + 1) % 16
    next_out = (o + 1) % 16
    source_x = (x + 1) % 4
    down_x = (x + 3) % 4
    down_to = zh * 4 + down_x
    down2_to = (zh * 4 + source_x + 2) % 16
    z_lo = o // 8
    wraps_y = jnp.logical_and(y == 3, c == 1)
    turns_y = jnp.logical_and(y < 2, c == 1)
    past_wrap = 8 - 8 * z_lo

    k_copy = pltpu.make_async_copy(k_hbm, k_ref, in_sem.at[0])
    v_copy = pltpu.make_async_copy(v_hbm, v_ref, in_sem.at[1])
    q_copy = pltpu.make_async_copy(q_hbm, q_ref, in_sem.at[2])
    k_copy.start()
    v_copy.start()
    q_copy.start()

    barrier = pltpu.get_barrier_semaphore()

    def greet(outer, inner):
        pl.semaphore_signal(barrier, inc=1, device_id=(outer, inner), device_id_type=MESH)

    greet(o, (i + 15) % 16)
    greet(o, zh * 4 + (x + 1) % 4)
    two_back = (i + 14) % 16
    greet(o, (two_back // 4) * 4 + (x + 1) % 4)
    greet((o + 15) % 16, i)

    @pl.when(x == 0)
    def _():
        greet(o, i + 3)
        greet(o, (i + 12) % 16)

    @pl.when(x == 1)
    def _():
        greet(o, (i + 13) % 16)

    @pl.when(turns_y)
    def _():
        greet(z_lo * 8 + 7, i)

    @pl.when(jnp.logical_and(y == 0, c == 0))
    def _():
        greet(past_wrap + 1, i)
        greet(past_wrap + 3, i)

    for which, codes, scale, copy in ((0, k_ref, kscale, k_copy), (1, v_ref, vscale, v_copy)):
        copy.wait()
        for h in range(KEY_HEADS):
            unit = jnp.where(formats[which, h] == 0, 1.0, 0.25)
            for s in range(2):
                part = codes[s * SPAN:(s + 1) * SPAN, h * SIZE:(h + 1) * SIZE].astype(jnp.float32)
                start = which * ROWS + s * SPAN
                kv[h, OWN, start:start + SPAN] = (part * (scale[s, h] * unit)).astype(jnp.bfloat16)

    peers = (
        4
        + jnp.where(jnp.logical_or(x == 0, x == 3), 1, 0)
        + jnp.where(turns_y, 1, 0)
        + jnp.where(x == 2, 1, 0)
        + jnp.where(wraps_y, 2, 0)
    )
    pl.semaphore_wait(barrier, peers)

    def send(h, source, target, flow, device, start=0, stop=BOTH):
        rows = pl.ds(start, stop - start)
        pltpu.make_async_remote_copy(
            kv.at[h, source, rows], kv.at[h, target, rows], sent.at[h, flow], recv.at[h, target],
            device_id=device, device_id_type=MESH,
        ).start()

    def arrived(h, slot, start=0, stop=BOTH):
        rows = pl.ds(start, stop - start)
        pltpu.make_async_copy(kv.at[h, slot, rows], kv.at[h, slot, rows], recv.at[h, slot]).wait()

    def left(h, flow, start=0, stop=BOTH):
        rows = pl.ds(start, stop - start)
        pltpu.make_async_copy(kv.at[h, OWN, rows], kv.at[h, OWN, rows], sent.at[h, flow]).wait()

    def send_in(h):
        @pl.when(x == 3)
        def _():
            send(h, OWN, VIA_Z, F_IN1, (o, i - 3), 0, FIRST)
            send(h, OWN, IN1, F_IN1, (o, next_in), FIRST, BOTH)

        @pl.when(x != 3)
        def _():
            send(h, OWN, IN1, F_IN1, (o, next_in))

        for at in range(4):
            @pl.when(x == at)
            def _():
                stop = HIGH if at == 2 else BOTH
                send(h, OWN, VIA_X, F_DOWN, (o, down_to), UP[at], stop)
                if at == 2:
                    send(h, OWN, VIA_X, F_DOWN, (o, (i + 3) % 16), HIGH, BOTH)

    def send_out(h):
        @pl.when(wraps_y)
        def _():
            send(h, OWN, VIA_Y, F_OUT0, (z_lo * 8 + 3, i))

        @pl.when(jnp.logical_not(wraps_y))
        def _():
            send(h, OWN, OUT0, F_OUT0, (next_out, i))

    def relay_wrap(h):
        @pl.when(x == 0)
        def _():
            arrived(h, VIA_Z, 0, FIRST)
            send(h, VIA_Z, IN1, F_WRAP, (o, (i + 4) % 16), 0, FIRST)

    def relay_down(h):
        for at in range(4):
            @pl.when(source_x == at)
            def _():
                stop = HIGH if at == 2 else BOTH
                arrived(h, VIA_X, UP[at], BOTH)
                send(h, VIA_X, IN2, F_DOWN2, (o, down2_to), UP[at], stop)
                if at == 2:
                    send(h, VIA_X, IN2, F_DOWN2, (o, i - 1), HIGH, BOTH)

    def relay_in1(h):
        arrived(h, IN1)
        for at in range(4):
            @pl.when(down_x == at)
            def _():
                send(h, IN1, IN2, F_UP2, (o, next_in), 0, UP[at])

        @pl.when(wraps_y)
        def _():
            send(h, IN1, VIA_Y, F_OUT1, (z_lo * 8 + 1, i))

        @pl.when(jnp.logical_not(wraps_y))
        def _():
            send(h, IN1, OUT1, F_OUT1, (next_out, i))

    def relay_in2(h):
        arrived(h, IN2)
        send(h, IN2, OUT2, F_OUT2, (next_out, i))

    def relay_y(h):
        @pl.when(jnp.logical_and(y == 0, c == 1))
        def _():
            arrived(h, VIA_Y)
            send(h, VIA_Y, OUT1, F_YWRAP, (past_wrap, i))

    def relay_y0(h):
        @pl.when(jnp.logical_and(y == 1, c == 1))
        def _():
            arrived(h, VIA_Y)
            send(h, VIA_Y, OUT0, F_YWRAP, (past_wrap, i))

    def out_copy(h):
        return pltpu.make_async_copy(
            o_ref.at[h],
            out_hbm.at[:, pl.ds(pl.multiple_of(h * (GROUP * SIZE), GROUP * SIZE), GROUP * SIZE)],
            o_sem.at[h],
        )

    def scores(h, g, first):
        columns = pl.ds(pl.multiple_of((h * GROUP + g) * SIZE, SIZE), SIZE)
        keys = kv[h, first:first + HALF, 0:ROWS].reshape(HALF * ROWS, SIZE)
        return lax.dot_general(
            q_ref[:, columns], keys, (((1,), (1,)), ((), ())),
            preferred_element_type=jnp.float32,
        ) + bias[:, first * ROWS:(first + HALF) * ROWS]

    def weighted(h, score, peak, first):
        expo = jnp.exp2((score - peak) * EXP_SCALE)
        values = kv[h, first:first + HALF, ROWS:BOTH].reshape(HALF * ROWS, SIZE)
        values = jnp.concatenate([values, jnp.ones((HALF * ROWS, SIZE), jnp.bfloat16)], axis=1)
        summed = jnp.dot(expo.astype(jnp.bfloat16), values, preferred_element_type=jnp.float32)
        return summed[:, :SIZE], summed[:, SIZE:]

    def attend_near(gs):
        def run(h):
            arrived(h, OUT0)

            @pl.when(h == 0)
            def _():
                q_copy.wait()

            for g in gs:
                score = scores(h, g, 0)
                peak = jnp.max(score, axis=1, keepdims=True)
                summed, total = weighted(h, score, peak, 0)
                sums[h, g] = summed
                peaks[h, g] = jnp.broadcast_to(peak, (ROWS, SIZE))
                totals[h, g] = total

        return run

    def attend_far(gs):
        def run(h):
            arrived(h, OUT1)
            arrived(h, OUT2)
            for g in gs:
                score = scores(h, g, HALF)
                near = peaks[h, g][:, 0:1]
                peak = jnp.maximum(near, jnp.max(score, axis=1, keepdims=True))
                summed, total = weighted(h, score, peak, HALF)
                keep = jnp.exp2((near - peak) * EXP_SCALE)
                result = (sums[h, g] * keep + summed) / (totals[h, g] * keep + total)
                o_ref[h, :, g * SIZE:(g + 1) * SIZE] = result.astype(jnp.bfloat16)
            out_copy(h).start()

        return run

    plan = plan_of(
        send_in, send_out, relay_wrap, relay_down, relay_in1, relay_in2, relay_y0, relay_y,
        attend_near, attend_far,
    )
    end = KEY_HEADS + max(lead for _, lead in plan)
    send_in(0)
    send_out(0)

    def step(t, carry):
        for stage, lead in plan:
            h = t - lead

            @pl.when(jnp.logical_and(h >= 0, h < KEY_HEADS))
            def _():
                stage(h)

        return carry

    below = lax.broadcasted_iota(jnp.int32, (SPAN, SPAN), 0)
    across = lax.broadcasted_iota(jnp.int32, (SPAN, SPAN), 1)
    for slot, (d_out, d_in) in enumerate(((0, 0), (1, 0), (0, 1), (0, 2), (1, 1), (1, 2))):
        block = ((o + 16 - d_out) % 16) * 16 + (i + 16 - d_in) % 16
        for s in range(2):
            key_at = order[block * 2 + s] * SPAN
            for r in range(2):
                query_at = order[(o * 16 + i) * 2 + r] * SPAN
                seen = key_at + across <= query_at + below
                bias[r * SPAN:(r + 1) * SPAN, (slot * 2 + s) * SPAN:(slot * 2 + s + 1) * SPAN] = (
                    jnp.where(seen, 0.0, -jnp.inf)
                )

    lax.fori_loop(0, end, step, 0)

    def finish(h, carry):
        out_copy(h).wait()
        for flow in (F_IN1, F_OUT0, F_OUT1, F_OUT2):
            left(h, flow)
        for at in range(4):
            @pl.when(x == at)
            def _():
                left(h, F_DOWN, UP[at], BOTH)

            @pl.when(source_x == at)
            def _():
                left(h, F_DOWN2, UP[at], BOTH)

            @pl.when(down_x == at)
            def _():
                left(h, F_UP2, 0, UP[at])

        @pl.when(x == 0)
        def _():
            left(h, F_WRAP, 0, FIRST)

        @pl.when(turns_y)
        def _():
            left(h, F_YWRAP)

        return carry

    lax.fori_loop(0, KEY_HEADS, finish, 0)


def shards(queries, key_codes, value_code_rows, key_scales, value_scales, formats, span_order):
    smem = pl.BlockSpec(memory_space=pltpu.SMEM)
    anywhere = pl.BlockSpec(memory_space=pl.ANY)
    flops = 4 * 32 * ROWS * SLOTS * ROWS * SIZE
    return pl.pallas_call(
        kernel,
        out_shape=jax.ShapeDtypeStruct((ROWS, KEY_HEADS * GROUP * SIZE), jnp.bfloat16),
        in_specs=[smem, smem, smem, smem, anywhere, anywhere, anywhere],
        out_specs=anywhere,
        scratch_shapes=[
            pltpu.VMEM((KEY_HEADS, 9, BOTH, SIZE), jnp.bfloat16),
            pltpu.VMEM((ROWS, SLOTS * ROWS), jnp.float32),
            pltpu.VMEM((KEY_HEADS, GROUP, ROWS, SIZE), jnp.float32),
            pltpu.VMEM((KEY_HEADS, GROUP, ROWS, SIZE), jnp.float32),
            pltpu.VMEM((KEY_HEADS, GROUP, ROWS, SIZE), jnp.float32),
            pltpu.VMEM((ROWS, KEY_HEADS * SIZE), jnp.bfloat16),
            pltpu.VMEM((ROWS, KEY_HEADS * SIZE), jnp.bfloat16),
            pltpu.VMEM((ROWS, KEY_HEADS * GROUP * SIZE), jnp.bfloat16),
            pltpu.VMEM((KEY_HEADS, ROWS, GROUP * SIZE), jnp.bfloat16),
            pltpu.SemaphoreType.DMA((KEY_HEADS, 9)),
            pltpu.SemaphoreType.DMA((KEY_HEADS, 9)),
            pltpu.SemaphoreType.DMA((3,)),
            pltpu.SemaphoreType.DMA((KEY_HEADS,)),
        ],
        compiler_params=pltpu.CompilerParams(
            collective_id=1, has_side_effects=True, vmem_limit_bytes=60 * 2**20
        ),
        cost_estimate=pl.CostEstimate(
            flops=flops, bytes_accessed=6 * 2**20, transcendentals=32 * ROWS * SLOTS * ROWS
        ),
        name="block_window_attention",
    )(key_scales, value_scales, formats, span_order, key_codes, value_code_rows, queries)


def solution(mesh):
    split = P(("outer", "inner"), None)
    return jax.shard_map(
        shards,
        mesh=mesh,
        in_specs=(split, split, split, split, split, P(), P()),
        out_specs=split,
        check_vma=False,
    )
```

time: 91.1 us -> 67.1 us (0.74)
  the two profiles are of different devices: /device:TPU:34 before, /device:TPU:1 now
where the time goes in v2:
time: 67.1 us; the launch traced here: 67 us
  Pallas kernels  63.9 us (95%)
  local copies, waits for them, and re-layouts  3.13 us (5%)
    pallas_call x1, Pallas kernels, shards(): pl.pallas_call(kernel, out_shape=jax.ShapeDtypeStruct((ROWS, KEY_HEADS *...  63.9 us
    unnamed x1, local copies, waits for them, and re-layouts  3.13 us

profile of v2, /device:TPU:1, one launch (start us, length us, event | category | flops | bytes accessed | tf_op | source)
XLA Modules:
  0.0 67.0 jit_solution(9305254088889502714)
XLA Ops:
  0.0 63.9 %block_window_attention.1 = bf16[256,4096]{1,0:T(8,128)(2,1)} custom-call(f32[2,8]{1,0:T(2,128)} %kscale.1, f32[2,8]{1,0:T(2,128)} %vscale.1, s32[2,8]{1,0:T(2,128)} %formats.1, s32[512]{0:T(512)} %order.1, bf16[256,1024]{1,0:T(8,128)(2,1)} %k_hbm.1, bf16[256,1024]{1,0:T(8,128)(2,1)} %v_hbm.1, bf16[256,4096]{1,0:T(8,128)(2,1)} %q_hbm.1), custom_call_target="tpu_custom_call" | custom-call | flops 6442450944 | bytes 6291456 | tf_op jit(solution)/shard_map/block_window_attention/pallas_call | solution.py:335
  63.9 3.1 %copy.9 = bf16[256,4096]{1,0:T(8,128)(2,1)} copy(bf16[256,4096]{1,0:T(8,128)(2,1)} %block_window_attention.1) | data formatting | bytes 4194304

commit v3 on v2

--- a/solution.py
+++ b/solution.py
@@ -27,14 +27,15 @@
 
 
 def plan_of(
-    send_in, send_out, relay_wrap, relay_down, relay_in1, relay_in2, relay_y0, relay_y,
+    send_via, send_in, send_out, relay_wrap, relay_down, relay_in1, relay_in2, relay_y0, relay_y,
     attend_near, attend_far
 ):
     return (
-        (send_in, -1),
+        (send_via, -2),
+        (send_in, -2),
         (relay_wrap, 1),
+        (relay_down, 1),
         (relay_y0, 1),
-        (relay_down, 1),
         (relay_in1, 2),
         (relay_in2, 3),
         (relay_y, 3),
@@ -135,23 +136,27 @@
         rows = pl.ds(start, stop - start)
         pltpu.make_async_copy(kv.at[h, OWN, rows], kv.at[h, OWN, rows], sent.at[h, flow]).wait()
 
+    def send_via(h):
+        @pl.when(x == 3)
+        def _():
+            send(h, OWN, VIA_Z, F_IN1, (o, i - 3), 0, FIRST)
+
+        for at in range(4):
+            @pl.when(x == at)
+            def _():
+                stop = HIGH if at == 2 else BOTH
+                if at == 2:
+                    send(h, OWN, VIA_X, F_DOWN, (o, (i + 3) % 16), HIGH, BOTH)
+                send(h, OWN, VIA_X, F_DOWN, (o, down_to), UP[at], stop)
+
     def send_in(h):
         @pl.when(x == 3)
         def _():
-            send(h, OWN, VIA_Z, F_IN1, (o, i - 3), 0, FIRST)
             send(h, OWN, IN1, F_IN1, (o, next_in), FIRST, BOTH)
 
         @pl.when(x != 3)
         def _():
             send(h, OWN, IN1, F_IN1, (o, next_in))
-
-        for at in range(4):
-            @pl.when(x == at)
-            def _():
-                stop = HIGH if at == 2 else BOTH
-                send(h, OWN, VIA_X, F_DOWN, (o, down_to), UP[at], stop)
-                if at == 2:
-                    send(h, OWN, VIA_X, F_DOWN, (o, (i + 3) % 16), HIGH, BOTH)
 
     def send_out(h):
         @pl.when(wraps_y)
@@ -266,12 +271,14 @@
         return run
 
     plan = plan_of(
-        send_in, send_out, relay_wrap, relay_down, relay_in1, relay_in2, relay_y0, relay_y,
+        send_via, send_in, send_out, relay_wrap, relay_down, relay_in1, relay_in2, relay_y0, relay_y,
         attend_near, attend_far,
     )
     end = KEY_HEADS + max(lead for _, lead in plan)
-    send_in(0)
-    send_out(0)
+    for t in range(min(lead for _, lead in plan), 0):
+        for stage, lead in plan:
+            if t - lead >= 0:
+                stage(t - lead)
 
     def step(t, carry):
         for stage, lead in plan:
@@ -334,7 +341,7 @@
     flops = 4 * 32 * ROWS * SLOTS * ROWS * SIZE
     return pl.pallas_call(
         kernel,
-        out_shape=jax.ShapeDtypeStruct((ROWS, KEY_HEADS * GROUP * SIZE), jnp.bfloat16),
+        out_shape=pltpu.VMEM((ROWS, KEY_HEADS * GROUP * SIZE), jnp.bfloat16),
         in_specs=[smem, smem, smem, smem, anywhere, anywhere, anywhere],
         out_specs=anywhere,
         scratch_shapes=[

time: 67.1 us -> 64.1 us (0.955)
  the two profiles are of different devices: /device:TPU:1 before, /device:TPU:34 now
where the time goes in v3:
time: 64.1 us; the launch traced here: 64 us
  Pallas kernels  62.6 us (98%)
  local copies, waits for them, and re-layouts  1.32 us (2%)
    pallas_call x1, Pallas kernels, shards(): pl.pallas_call(kernel, out_shape=pltpu.VMEM((ROWS, KEY_HEADS * GROUP * SI...  62.6 us
    unnamed x1, local copies, waits for them, and re-layouts  1.32 us

profile of v3, /device:TPU:34, one launch (start us, length us, event | category | flops | bytes accessed | tf_op | source)
XLA Modules:
  0.0 64.0 jit_solution(291682138044622368)
XLA Ops:
  0.0 62.6 %block_window_attention.1 = bf16[256,4096]{1,0:T(8,128)(2,1)S(1)} custom-call(f32[2,8]{1,0:T(2,128)} %kscale.1, f32[2,8]{1,0:T(2,128)} %vscale.1, s32[2,8]{1,0:T(2,128)} %formats.1, s32[512]{0:T(512)} %order.1, bf16[256,1024]{1,0:T(8,128)(2,1)} %k_hbm.1, bf16[256,1024]{1,0:T(8,128)(2,1)} %v_hbm.1, bf16[256,4096]{1,0:T(8,128)(2,1)} %q_hbm.1), custom_call_target="tpu_custom_call" | custom-call | flops 6442450944 | bytes 6291456 | tf_op jit(solution)/shard_map/block_window_attention/pallas_call | solution.py:342
  62.6 1.3 %copy.9 = bf16[256,4096]{1,0:T(8,128)(2,1)} copy(bf16[256,4096]{1,0:T(8,128)(2,1)S(1)} %block_window_attention.1) | data formatting | bytes 4194304

commit v4 on v3

--- a/solution.py
+++ b/solution.py
@@ -17,18 +17,21 @@
 HALF = 3
 EXP_SCALE = math.log2(math.e) / math.sqrt(SIZE)
 
-OWN, OUT0, IN1, IN2, OUT1, OUT2, VIA_Z, VIA_X, VIA_Y = range(9)
-F_IN1, F_DOWN, F_OUT0, F_WRAP, F_DOWN2, F_UP2, F_OUT1, F_OUT2, F_YWRAP = range(9)
-
-UP = (128, 256, 80, 352)
-HIGH = 384
+OWN, OUT0, IN1, IN2, OUT1, OUT2, VIA_Z, VIA_X, VIA_Y, VIA_Y2 = range(10)
+LATE_Y = 10
+F_IN1, F_DOWN, F_OUT0, F_WRAP, F_DOWN2, F_UP2, F_OUT1, F_OUT2, F_YWRAP, F_YWRAP2 = range(10)
+
+UP = (128, 256, 80, 304)
+HIGH = 400
 FIRST = 304
 BOTH = 2 * ROWS
+QUARTER = 128
+MOST = 384
 
 
 def plan_of(
-    send_via, send_in, send_out, relay_wrap, relay_down, relay_in1, relay_in2, relay_y0, relay_y,
-    attend_near, attend_far
+    send_via, send_in, send_out, relay_wrap, relay_down, relay_in1, relay_in2,
+    relay_y0, relay_y1, relay_y, relay_y2, attend_near, attend_far
 ):
     return (
         (send_via, -2),
@@ -39,6 +42,8 @@
         (relay_in1, 2),
         (relay_in2, 3),
         (relay_y, 3),
+        (relay_y1, 2),
+        (relay_y2, 4),
         (send_out, -1),
         (attend_near(range(GROUP)), 3),
         (attend_far(range(GROUP)), 4),
@@ -64,7 +69,8 @@
     down2_to = (zh * 4 + source_x + 2) % 16
     z_lo = o // 8
     wraps_y = jnp.logical_and(y == 3, c == 1)
-    turns_y = jnp.logical_and(y < 2, c == 1)
+    turns_y = jnp.logical_and(y < 3, c == 1)
+    turns_at = [jnp.logical_and(y == at, c == 1) for at in range(3)]
     past_wrap = 8 - 8 * z_lo
 
     k_copy = pltpu.make_async_copy(k_hbm, k_ref, in_sem.at[0])
@@ -102,6 +108,11 @@
     def _():
         greet(past_wrap + 1, i)
         greet(past_wrap + 3, i)
+        greet(z_lo * 8 + 3, i)
+
+    @pl.when(turns_at[1])
+    def _():
+        greet(past_wrap + 5, i)
 
     for which, codes, scale, copy in ((0, k_ref, kscale, k_copy), (1, v_ref, vscale, v_copy)):
         copy.wait()
@@ -116,21 +127,26 @@
         4
         + jnp.where(jnp.logical_or(x == 0, x == 3), 1, 0)
         + jnp.where(turns_y, 1, 0)
+        + jnp.where(turns_at[1], 1, 0)
         + jnp.where(x == 2, 1, 0)
-        + jnp.where(wraps_y, 2, 0)
+        + jnp.where(wraps_y, 3, 0)
     )
     pl.semaphore_wait(barrier, peers)
 
-    def send(h, source, target, flow, device, start=0, stop=BOTH):
+    def send(h, source, target, flow, device, start=0, stop=BOTH, signal=None):
         rows = pl.ds(start, stop - start)
         pltpu.make_async_remote_copy(
-            kv.at[h, source, rows], kv.at[h, target, rows], sent.at[h, flow], recv.at[h, target],
+            kv.at[h, source, rows], kv.at[h, target, rows], sent.at[h, flow],
+            recv.at[h, target if signal is None else signal],
             device_id=device, device_id_type=MESH,
         ).start()
 
-    def arrived(h, slot, start=0, stop=BOTH):
+    def arrived(h, slot, start=0, stop=BOTH, signal=None):
         rows = pl.ds(start, stop - start)
-        pltpu.make_async_copy(kv.at[h, slot, rows], kv.at[h, slot, rows], recv.at[h, slot]).wait()
+        pltpu.make_async_copy(
+            kv.at[h, slot, rows], kv.at[h, slot, rows],
+            recv.at[h, slot if signal is None else signal],
+        ).wait()
 
     def left(h, flow, start=0, stop=BOTH):
         rows = pl.ds(start, stop - start)
@@ -161,7 +177,8 @@
     def send_out(h):
         @pl.when(wraps_y)
         def _():
-            send(h, OWN, VIA_Y, F_OUT0, (z_lo * 8 + 3, i))
+            send(h, OWN, VIA_Y, F_OUT0, (z_lo * 8 + 5, i), QUARTER, BOTH)
+            send(h, OWN, VIA_Y, F_OUT0, (z_lo * 8 + 3, i), 0, QUARTER)
 
         @pl.when(jnp.logical_not(wraps_y))
         def _():
@@ -192,7 +209,8 @@
 
         @pl.when(wraps_y)
         def _():
-            send(h, IN1, VIA_Y, F_OUT1, (z_lo * 8 + 1, i))
+            send(h, IN1, VIA_Y, F_OUT1, (z_lo * 8 + 1, i), 0, ROWS)
+            send(h, IN1, VIA_Y, F_OUT1, (z_lo * 8 + 3, i), ROWS, BOTH, LATE_Y)
 
         @pl.when(jnp.logical_not(wraps_y))
         def _():
@@ -200,19 +218,49 @@
 
     def relay_in2(h):
         arrived(h, IN2)
-        send(h, IN2, OUT2, F_OUT2, (next_out, i))
+
+        @pl.when(wraps_y)
+        def _():
+            send(h, IN2, VIA_Y, F_OUT2, (z_lo * 8 + 1, i), MOST, BOTH, LATE_Y)
+            send(h, IN2, OUT2, F_OUT2, (past_wrap, i), 0, MOST)
+
+        @pl.when(jnp.logical_not(wraps_y))
+        def _():
+            send(h, IN2, OUT2, F_OUT2, (next_out, i))
+
+    def relay_y0(h):
+        @pl.when(turns_at[1])
+        def _():
+            arrived(h, VIA_Y, 0, QUARTER)
+            send(h, VIA_Y, OUT0, F_YWRAP, (past_wrap, i), 0, QUARTER)
+
+        @pl.when(turns_at[2])
+        def _():
+            arrived(h, VIA_Y, QUARTER, BOTH)
+            send(h, VIA_Y, VIA_Y2, F_YWRAP, (past_wrap + 3, i), QUARTER, BOTH)
+
+    def relay_y1(h):
+        @pl.when(turns_at[1])
+        def _():
+            arrived(h, VIA_Y2, QUARTER, BOTH)
+            send(h, VIA_Y2, OUT0, F_YWRAP2, (z_lo * 8, i), QUARTER, BOTH)
 
     def relay_y(h):
-        @pl.when(jnp.logical_and(y == 0, c == 1))
-        def _():
-            arrived(h, VIA_Y)
-            send(h, VIA_Y, OUT1, F_YWRAP, (past_wrap, i))
-
-    def relay_y0(h):
-        @pl.when(jnp.logical_and(y == 1, c == 1))
-        def _():
-            arrived(h, VIA_Y)
-            send(h, VIA_Y, OUT0, F_YWRAP, (past_wrap, i))
+        @pl.when(turns_at[0])
+        def _():
+            arrived(h, VIA_Y, 0, ROWS)
+            send(h, VIA_Y, OUT1, F_YWRAP, (past_wrap, i), 0, ROWS)
+
+        @pl.when(turns_at[1])
+        def _():
+            arrived(h, VIA_Y, ROWS, BOTH, LATE_Y)
+            send(h, VIA_Y, OUT1, F_YWRAP, (past_wrap, i), ROWS, BOTH)
+
+    def relay_y2(h):
+        @pl.when(turns_at[0])
+        def _():
+            arrived(h, VIA_Y, MOST, BOTH, LATE_Y)
+            send(h, VIA_Y, OUT2, F_YWRAP, (past_wrap, i), MOST, BOTH)
 
     def out_copy(h):
         return pltpu.make_async_copy(
@@ -271,7 +319,7 @@
         return run
 
     plan = plan_of(
-        send_via, send_in, send_out, relay_wrap, relay_down, relay_in1, relay_in2, relay_y0, relay_y,
+        send_via, send_in, send_out, relay_wrap, relay_down, relay_in1, relay_in2, relay_y0, relay_y1, relay_y, relay_y2,
         attend_near, attend_far,
     )
     end = KEY_HEADS + max(lead for _, lead in plan)
@@ -328,7 +376,11 @@
 
         @pl.when(turns_y)
         def _():
-            left(h, F_YWRAP)
+            left(h, F_YWRAP, 0, MOST)
+
+        @pl.when(turns_at[1])
+        def _():
+            left(h, F_YWRAP2, 0, MOST)
 
         return carry
 
@@ -345,7 +397,7 @@
         in_specs=[smem, smem, smem, smem, anywhere, anywhere, anywhere],
         out_specs=anywhere,
         scratch_shapes=[
-            pltpu.VMEM((KEY_HEADS, 9, BOTH, SIZE), jnp.bfloat16),
+            pltpu.VMEM((KEY_HEADS, 10, BOTH, SIZE), jnp.bfloat16),
             pltpu.VMEM((ROWS, SLOTS * ROWS), jnp.float32),
             pltpu.VMEM((KEY_HEADS, GROUP, ROWS, SIZE), jnp.float32),
             pltpu.VMEM((KEY_HEADS, GROUP, ROWS, SIZE), jnp.float32),
@@ -354,8 +406,8 @@
             pltpu.VMEM((ROWS, KEY_HEADS * SIZE), jnp.bfloat16),
             pltpu.VMEM((ROWS, KEY_HEADS * GROUP * SIZE), jnp.bfloat16),
             pltpu.VMEM((KEY_HEADS, ROWS, GROUP * SIZE), jnp.bfloat16),
-            pltpu.SemaphoreType.DMA((KEY_HEADS, 9)),
-            pltpu.SemaphoreType.DMA((KEY_HEADS, 9)),
+            pltpu.SemaphoreType.DMA((KEY_HEADS, 11)),
+            pltpu.SemaphoreType.DMA((KEY_HEADS, 10)),
             pltpu.SemaphoreType.DMA((3,)),
             pltpu.SemaphoreType.DMA((KEY_HEADS,)),
         ],

time: 64.1 us -> 65.7 us (1.025)
  Pallas kernels: 62.6 us -> 64.3 us
    pallas_call x1, Pallas kernels: 62.6 us -> 64.3 us  [shards(): pl.pallas_call(kernel, out_shape=pltpu.VMEM((ROWS, KEY_HEADS * GROUP * SI...]
where the time goes in v4:
time: 65.7 us; the launch traced here: 65.6 us
  Pallas kernels  64.3 us (98%)
  local copies, waits for them, and re-layouts  1.32 us (2%)
    pallas_call x1, Pallas kernels, shards(): pl.pallas_call(kernel, out_shape=pltpu.VMEM((ROWS, KEY_HEADS * GROUP * SI...  64.3 us
    unnamed x1, local copies, waits for them, and re-layouts  1.32 us

profile of v4, /device:TPU:34, one launch (start us, length us, event | category | flops | bytes accessed | tf_op | source)
XLA Modules:
  0.0 65.6 jit_solution(158783516564636422)
XLA Ops:
  0.0 64.3 %block_window_attention.1 = bf16[256,4096]{1,0:T(8,128)(2,1)S(1)} custom-call(f32[2,8]{1,0:T(2,128)} %kscale.1, f32[2,8]{1,0:T(2,128)} %vscale.1, s32[2,8]{1,0:T(2,128)} %formats.1, s32[512]{0:T(512)} %order.1, bf16[256,1024]{1,0:T(8,128)(2,1)} %k_hbm.1, bf16[256,1024]{1,0:T(8,128)(2,1)} %v_hbm.1, bf16[256,4096]{1,0:T(8,128)(2,1)} %q_hbm.1), custom_call_target="tpu_custom_call" | custom-call | flops 6442450944 | bytes 6291456 | tf_op jit(solution)/shard_map/block_window_attention/pallas_call | solution.py:394
  64.3 1.3 %copy.9 = bf16[256,4096]{1,0:T(8,128)(2,1)} copy(bf16[256,4096]{1,0:T(8,128)(2,1)S(1)} %block_window_attention.1) | data formatting | bytes 4194304

commit v5 on v3

--- a/solution.py
+++ b/solution.py
@@ -20,6 +20,7 @@
 OWN, OUT0, IN1, IN2, OUT1, OUT2, VIA_Z, VIA_X, VIA_Y = range(9)
 F_IN1, F_DOWN, F_OUT0, F_WRAP, F_DOWN2, F_UP2, F_OUT1, F_OUT2, F_YWRAP = range(9)
 
+FIRST_SENT = 2
 UP = (128, 256, 80, 352)
 HIGH = 384
 FIRST = 304
@@ -28,7 +29,7 @@
 
 def plan_of(
     send_via, send_in, send_out, relay_wrap, relay_down, relay_in1, relay_in2, relay_y0, relay_y,
-    attend_near, attend_far
+    attend_near, attend_far, finish
 ):
     return (
         (send_via, -2),
@@ -42,6 +43,7 @@
         (send_out, -1),
         (attend_near(range(GROUP)), 3),
         (attend_far(range(GROUP)), 4),
+        (finish, 5),
     )
 
 
@@ -103,14 +105,18 @@
         greet(past_wrap + 1, i)
         greet(past_wrap + 3, i)
 
-    for which, codes, scale, copy in ((0, k_ref, kscale, k_copy), (1, v_ref, vscale, v_copy)):
-        copy.wait()
-        for h in range(KEY_HEADS):
+    def dequantize(h):
+        for which, codes, scale in ((0, k_ref, kscale), (1, v_ref, vscale)):
             unit = jnp.where(formats[which, h] == 0, 1.0, 0.25)
             for s in range(2):
                 part = codes[s * SPAN:(s + 1) * SPAN, h * SIZE:(h + 1) * SIZE].astype(jnp.float32)
                 start = which * ROWS + s * SPAN
                 kv[h, OWN, start:start + SPAN] = (part * (scale[s, h] * unit)).astype(jnp.bfloat16)
+
+    k_copy.wait()
+    v_copy.wait()
+    for h in range(FIRST_SENT):
+        dequantize(h)
 
     peers = (
         4
@@ -270,15 +276,43 @@
 
         return run
 
+    def finish(h):
+        out_copy(h).wait()
+        for flow in (F_IN1, F_OUT0, F_OUT1, F_OUT2):
+            left(h, flow)
+        for at in range(4):
+            @pl.when(x == at)
+            def _():
+                left(h, F_DOWN, UP[at], BOTH)
+
+            @pl.when(source_x == at)
+            def _():
+                left(h, F_DOWN2, UP[at], BOTH)
+
+            @pl.when(down_x == at)
+            def _():
+                left(h, F_UP2, 0, UP[at])
+
+        @pl.when(x == 0)
+        def _():
+            left(h, F_WRAP, 0, FIRST)
+
+        @pl.when(turns_y)
+        def _():
+            left(h, F_YWRAP)
+
     plan = plan_of(
         send_via, send_in, send_out, relay_wrap, relay_down, relay_in1, relay_in2, relay_y0, relay_y,
-        attend_near, attend_far,
+        attend_near, attend_far, finish,
     )
     end = KEY_HEADS + max(lead for _, lead in plan)
     for t in range(min(lead for _, lead in plan), 0):
         for stage, lead in plan:
             if t - lead >= 0:
                 stage(t - lead)
+
+    for h in range(FIRST_SENT, KEY_HEADS):
+        dequantize(h)
 
     def step(t, carry):
         for stage, lead in plan:
@@ -304,35 +338,6 @@
                 )
 
     lax.fori_loop(0, end, step, 0)
-
-    def finish(h, carry):
-        out_copy(h).wait()
-        for flow in (F_IN1, F_OUT0, F_OUT1, F_OUT2):
-            left(h, flow)
-        for at in range(4):
-            @pl.when(x == at)
-            def _():
-                left(h, F_DOWN, UP[at], BOTH)
-
-            @pl.when(source_x == at)
-            def _():
-                left(h, F_DOWN2, UP[at], BOTH)
-
-            @pl.when(down_x == at)
-            def _():
-                left(h, F_UP2, 0, UP[at])
-
-        @pl.when(x == 0)
-        def _():
-            left(h, F_WRAP, 0, FIRST)
-
-        @pl.when(turns_y)
-        def _():
-            left(h, F_YWRAP)
-
-        return carry
-
-    lax.fori_loop(0, KEY_HEADS, finish, 0)
 
 
 def shards(queries, key_codes, value_code_rows, key_scales, value_scales, formats, span_order):

time: 64.1 us -> 63.8 us (level)
  no operation moved by 1% of the time
where the time goes in v5:
time: 63.8 us; the launch traced here: 63.7 us
  Pallas kernels  62.3 us (98%)
  local copies, waits for them, and re-layouts  1.32 us (2%)
    pallas_call x1, Pallas kernels, shards(): pl.pallas_call(kernel, out_shape=pltpu.VMEM((ROWS, KEY_HEADS * GROUP * SI...  62.3 us
    unnamed x1, local copies, waits for them, and re-layouts  1.32 us

profile of v5, /device:TPU:34, one launch (start us, length us, event | category | flops | bytes accessed | tf_op | source)
XLA Modules:
  0.0 63.7 jit_solution(15709824274602087434)
XLA Ops:
  0.0 62.3 %block_window_attention.1 = bf16[256,4096]{1,0:T(8,128)(2,1)S(1)} custom-call(f32[2,8]{1,0:T(2,128)} %kscale.1, f32[2,8]{1,0:T(2,128)} %vscale.1, s32[2,8]{1,0:T(2,128)} %formats.1, s32[512]{0:T(512)} %order.1, bf16[256,1024]{1,0:T(8,128)(2,1)} %k_hbm.1, bf16[256,1024]{1,0:T(8,128)(2,1)} %v_hbm.1, bf16[256,4096]{1,0:T(8,128)(2,1)} %q_hbm.1), custom_call_target="tpu_custom_call" | custom-call | flops 6442450944 | bytes 6291456 | tf_op jit(solution)/shard_map/block_window_attention/pallas_call | solution.py:347
  62.3 1.3 %copy.9 = bf16[256,4096]{1,0:T(8,128)(2,1)} copy(bf16[256,4096]{1,0:T(8,128)(2,1)S(1)} %block_window_attention.1) | data formatting | bytes 4194304
